TPU v7x, 32 devices: a whole 2x2x4 slice. The times are simulated.
32 devices in a mesh: tm: 4 (over y, x), chan: 8 (over z, core).
Axes of the slice: x: 2, y: 2, z: 4, core: 2. Of those that a mesh axis runs over, the one named last changes fastest.
Arguments:
- voltages: bfloat16 [2, 128, 2048, 1024], P(None, 'tm', 'chan'), may hold values from -6 to 6
- subspace: float32 [8, 256, 32, 1024], P('chan', 'tm'), may hold values from -0.1875 to 0.1875
- order: int32 [256], replicated, may hold values from 0 to 255, each once
- beam_seeds: int32 [256], replicated, may hold values from 1 to 65520
- flagged: int32 [16], replicated, may hold values from 0 to 511
Outputs:
- beams: bfloat16 [2, 8, 256, 512, 128], P(None, None, 'tm', 'chan')
- tracked: float32 [8, 256, 32, 1024], P('chan', 'tm')
Inputs may be any that keep to these rules, and one draw needn't show every extreme that they name: `order`: each of 0 to 255 once. `flagged`: station numbers; a station may occur more than once.
All inputs are finite; a program needn't handle non-finite values.
Results may differ from a plain program's by a relative error of at most 0.0084.
Values may be sent and summed in bfloat16 or wider, within the bound.
A program may use at most 256 MiB of HBM per device.

v0:
```python
import math

import jax
import jax.numpy as jnp
from jax import lax
from jax.sharding import PartitionSpec as P

CH = 2048
SUB = 2


TWO_PI = 2.0 * math.pi


def beam_weights(beam_seeds, channels, stations, total_channels):
    station_no = jnp.arange(stations, dtype=jnp.int32) + 1
    delays = (station_no[:, None] * beam_seeds[None, :] % 65521).astype(jnp.float32) / 65521.0
    frequency = 1.0 + channels.astype(jnp.float32) / total_channels
    angles = delays[None, :, :] * (TWO_PI * frequency)[:, None, None]
    factor = 1.0 / math.sqrt(stations)
    cosine = jnp.cos(angles) * factor
    sine_part = jnp.sin(angles) * factor
    upper = jnp.concatenate([cosine, sine_part], axis=2)
    under = jnp.concatenate([-sine_part, cosine], axis=2)
    return jnp.concatenate([upper, under], axis=1).astype(jnp.bfloat16)


def power_step(voltage_input, tracked, steering_weight):
    sample_count = voltage_input.shape[0]
    coarse_channel = tracked.astype(jnp.bfloat16)
    projected_input = jnp.einsum(
        "xbj,bqj->bxq", voltage_input, coarse_channel, preferred_element_type=jnp.float32
    ).astype(jnp.bfloat16)
    beam_image = (
        jnp.einsum(
            "nwg,wny->ngy", projected_input, voltage_input, preferred_element_type=jnp.float32
        )
        + sample_count * tracked
    )
    gram = jnp.einsum("crs,cks->crk", beam_image, beam_image, precision=lax.Precision.HIGHEST)
    lower = jnp.linalg.cholesky(gram)
    tracked = jax.scipy.linalg.solve_triangular(lower, beam_image, lower=True)
    subspace_vectors = tracked.astype(jnp.bfloat16)
    lengthwise_axis = jnp.einsum(
        "xbj,bqj->bxq", voltage_input, subspace_vectors, preferred_element_type=jnp.float32
    ).astype(jnp.bfloat16)
    mixing = jnp.einsum(
        "crs,csb->crb", subspace_vectors, steering_weight, preferred_element_type=jnp.float32
    ).astype(jnp.bfloat16)
    direct_output = jnp.einsum(
        "edi,diy->dye", voltage_input, steering_weight, preferred_element_type=jnp.float32
    )
    beams = direct_output - jnp.einsum(
        "ctr,crb->cbt", lengthwise_axis, mixing, preferred_element_type=jnp.float32
    )
    return (tracked, beams.astype(jnp.bfloat16))


def per_device(voltages, subspace, order, beam_seeds, flagged):
    signals = voltages.shape[-1]
    stations = signals // 2
    slots = subspace.shape[1]
    per_group = order.shape[0]
    marks = jnp.any(flagged[:, None] == jnp.arange(stations, dtype=jnp.int32)[None, :], axis=0)
    keep = jnp.where(marks, 0.0, 1.0).astype(jnp.bfloat16)
    keep = jnp.concatenate([keep, keep])
    ordered = jnp.take(voltages, order, axis=2) * keep
    group = lax.axis_index("chan")
    first_slot = lax.axis_index("tm") * slots
    chosen = lax.dynamic_slice_in_dim(order, first_slot, slots)
    channels = group * per_group + chosen
    steering_weight = beam_weights(beam_seeds, channels, stations, CH)
    state = subspace[0]
    results = []
    for part in range(SUB):
        turned = lax.all_to_all(ordered[part], "tm", split_axis=1, concat_axis=0, tiled=True)
        state, formed = power_step(turned, state, steering_weight)
        results.append(
            lax.all_to_all(formed[None], "chan", split_axis=2, concat_axis=0, tiled=True)
        )
    output = jnp.stack(results)
    return (output, state[None])


def solution(mesh):
    return jax.shard_map(
        per_device,
        mesh=mesh,
        in_specs=(P(None, "tm", "chan", None), P("chan", "tm", None, None), P(), P(), P()),
        out_specs=(P(None, None, "tm", "chan", None), P("chan", "tm", None, None)),
        check_vma=False,
    )
```

profile of v0, /device:TPU:0, one launch (start us, length us, event | category | flops | bytes accessed | tf_op | source)
XLA Modules:
  0.0 1297.3 jit_solution(2025269014497460757)
XLA Ops:
  2.8 61.8 %gather_fusion = bf16[256,2,32,1024]{3,0,2,1:T(8,128)(2,1)} fusion(bf16[2,32,256,1024]{3,2,1,0:T(8,128)(2,1)} %param.8, s32[1024]{0:T(1024)S(1)} %pad_clamp_fusion), kind=kCustom, calls=%fused_computation | custom fusion | bytes 67109888 | tf_op jit(solution)/shard_map/jit(_take)/gather | solution.py:67
  64.6 22.9 %multiply_bitcast_fusion = bf16[2,32,256,1024]{3,2,1,0:T(8,128)(2,1)} fusion(bf16[256,2,32,1024]{3,0,2,1:T(8,128)(2,1)} %gather_fusion, pred[256]{0:T(512)(128)(4,1)S(1)} %compare_and_fusion, bf16[1024]{0:T(1024)(128)(2,1)S(1)} %pad_maximum_fusion.1), kind=kLoop, calls=%fused_computation.10 | loop fusion | flops 33554432 | bytes 67111168 | tf_op jit(solution)/shard_map/mul | solution.py:67
  87.5 18.2 %slice_bitcast_fusion.1 = (bf16[32,256,1024]{2,1,0:T(8,128)(2,1)S(1)}, bf16[32,256,1024]{2,1,0:T(8,128)(2,1)}) fusion(bf16[2,32,256,1024]{3,2,1,0:T(8,128)(2,1)} %multiply_bitcast_fusion), kind=kLoop, calls=%fused_computation.12 | loop fusion | bytes 67108864 | tf_op jit(solution)/shard_map/squeeze | solution.py:76
  105.7 24.7 %copy.49 = bf16[32,256,1024]{2,0,1:T(8,128)(2,1)} copy(bf16[32,256,1024]{2,1,0:T(8,128)(2,1)S(1)} %get-tuple-element.4) | data formatting | bytes 33554432 | tf_op jit(solution)/shard_map/squeeze | solution.py:76
  137.7 18.7 %copy.58 = bf16[32,256,1024]{2,0,1:T(8,128)(2,1)} copy(bf16[32,256,1024]{2,1,0:T(8,128)(2,1)} %get-tuple-element.5) | data formatting | bytes 33554432 | tf_op jit(solution)/shard_map/squeeze | solution.py:76
  156.9 126.4 %fusion.4 = (bf16[64,512,256]{1,2,0:T(8,128)(2,1)}, bf16[64,512,256]{1,2,0:T(8,128)(2,1)}, bf16[64,512,256]{1,2,0:T(8,128)(2,1)}) fusion(f32[64]{0:T(128)S(1)} %add_multiply_fusion, f32[512,256]{0,1:T(8,128)S(1)} %fusion.32), kind=kLoop, calls=%fused_computation.8 | loop fusion | flops 58720256 | bytes 50856192 | tf_op jit(solution)/shard_map/convert.5
  283.3 38.1 %all-to-all-done = bf16[32,256,1024]{2,0,1:T(8,128)(2,1)} async-done(((bf16[32,256,1024]{2,0,1:T(8,128)(2,1)}), bf16[32,256,1024]{2,0,1:T(8,128)(2,1)}, u32[]{:S(2)}, u32[]{:S(2)}) %all-to-all-start) | async-done | bytes 16777248 | tf_op jit(solution)/shard_map/all_to_all | solution.py:76
  328.8 14.3 %copy.50 = bf16[32,4,64,1024]{3,0,1,2:T(8,128)(2,1)} copy(bf16[32,4,64,1024]{3,0,2,1:T(8,128)(2,1)} %bitcast.2) | data formatting | bytes 33554432 | tf_op jit(solution)/shard_map/all_to_all | solution.py:76
  343.0 25.7 %bitcast_add_fusion = f32[64,32,1024]{2,1,0:T(8,128)} fusion(f32[1,64,32,1024]{3,2,1,0:T(8,128)} %param.9, bf16[128,64,1024]{2,0,1:T(8,128)(2,1)} %bitcast.80), kind=kOutput, calls=%fused_computation.16 | convolution fusion | flops 1080295424 | bytes 33554432 | tf_op jit(solution)/shard_map/nwg,wny->ngy/dot_general | solution.py:35
  368.8 13.6 %fusion.44 = f32[64,32,32]{2,1,0:T(8,128)S(1)} fusion(f32[64,32,1024]{2,1,0:T(8,128)} %bitcast_add_fusion), kind=kOutput, calls=%fused_computation.69 | convolution fusion | flops 805306368 | bytes 8650752 | tf_op jit(solution)/shard_map/crs,cks->crk/dot_general | solution.py:40
  382.9 187.5 %custom-call.8 = f32[64,32,32]{2,1,0:T(8,128)S(1)} custom-call(f32[64,32,32]{2,1,0:T(8,128)S(1)} %fusion.30), custom_call_target="Cholesky" | custom-call | tf_op jit(solution)/shard_map/jit(cholesky)/cholesky | solution.py:41
  571.5 12.5 custom-call.9
  584.9 11.9 fusion.45
  596.8 30.4 %fusion.73 = bf16[64,32,512]{2,1,0:T(8,128)(2,1)S(1)} fusion(f32[64,32,1024]{2,1,0:T(8,128)} %fusion.45, bf16[64,512,256]{1,2,0:T(8,128)(2,1)} %get-tuple-element.8, bf16[64,512,256]{1,2,0:T(8,128)(2,1)} %get-tuple-element.7, bf16[64,512,256]{1,2,0:T(8,128)(2,1)} %get-tuple-element.6), kind=kOutput, calls=%fused_computation.30.clone.1 | convolution fusion | flops 2419064832 | bytes 60817408 | tf_op jit(solution)/shard_map/crs,csb->crb/dot_general | solution.py:47
  627.3 11.1 convolution_convert_fusion.1
  638.4 37.0 %fusion.43 = f32[64,512,128]{2,1,0:T(8,128)} fusion(bf16[128,64,1024]{2,0,1:T(8,128)(2,1)} %bitcast.82, bf16[64,512,256]{1,2,0:T(8,128)(2,1)} %get-tuple-element.8, bf16[64,512,256]{1,2,0:T(8,128)(2,1)} %get-tuple-element.7, bf16[64,512,256]{1,2,0:T(8,128)(2,1)} %get-tuple-element.6), kind=kOutput, calls=%fused_computation.68 | convolution fusion | flops 8858370048 | bytes 83886080 | tf_op jit(solution)/shard_map/edi,diy->dye/dot_general | solution.py:50
  675.4 9.4 fusion.6
  684.8 12.1 copy.56
  702.3 14.3 %copy.59 = bf16[32,4,64,1024]{3,0,1,2:T(8,128)(2,1)} copy(bf16[32,4,64,1024]{3,0,2,1:T(8,128)(2,1)} %bitcast.16) | data formatting | bytes 33554432 | tf_op jit(solution)/shard_map/all_to_all | solution.py:76
  716.6 25.5 %multiply_add_fusion = f32[64,32,1024]{2,1,0:T(8,128)} fusion(f32[64,32,1024]{2,1,0:T(8,128)} %fusion.45, bf16[128,64,1024]{2,0,1:T(8,128)(2,1)} %bitcast.77), kind=kOutput, calls=%fused_computation.19 | convolution fusion | flops 1080295424 | bytes 33554432 | tf_op jit(solution)/shard_map/nwg,wny->ngy/dot_general | solution.py:35
  742.1 13.6 %fusion.46 = f32[64,32,32]{2,1,0:T(8,128)S(1)} fusion(f32[64,32,1024]{2,1,0:T(8,128)} %multiply_add_fusion), kind=kOutput, calls=%fused_computation.71 | convolution fusion | flops 805306368 | bytes 8650752 | tf_op jit(solution)/shard_map/crs,cks->crk/dot_general | solution.py:40
  756.2 187.5 %custom-call.10 = f32[64,32,32]{2,1,0:T(8,128)S(1)} custom-call(f32[64,32,32]{2,1,0:T(8,128)S(1)} %fusion.29), custom_call_target="Cholesky" | custom-call | tf_op jit(solution)/shard_map/jit(cholesky)/cholesky | solution.py:41
  944.8 12.5 custom-call.11
  958.2 23.0 %fusion.47 = f32[64,32,1024]{2,1,0:T(8,128)} fusion(f32[64,32,32]{2,1,0:T(8,128)S(1)} %copy.63, f32[64,32,1024]{2,1,0:T(8,128)} %multiply_add_fusion), kind=kOutput, calls=%fused_computation.72 | convolution fusion | flops 805306368 | bytes 17039360 | tf_op jit(solution)/shard_map/jit(_solve_triangular)/vmap()/triangular_solve | solution.py:42
  981.3 11.9 fusion.21
  993.1 30.4 %fusion.76 = bf16[64,32,512]{2,1,0:T(8,128)(2,1)S(1)} fusion(f32[64,32,1024]{2,1,0:T(8,128)} %fusion.47, bf16[64,512,256]{1,2,0:T(8,128)(2,1)} %get-tuple-element.8, bf16[64,512,256]{1,2,0:T(8,128)(2,1)} %get-tuple-element.7, bf16[64,512,256]{1,2,0:T(8,128)(2,1)} %get-tuple-element.6), kind=kOutput, calls=%fused_computation.25.clone | convolution fusion | flops 2419064832 | bytes 60817408 | tf_op jit(solution)/shard_map/crs,csb->crb/dot_general | solution.py:47
  1023.6 37.1 %fusion.42 = f32[64,512,128]{2,1,0:T(8,128)} fusion(bf16[128,64,1024]{2,0,1:T(8,128)(2,1)} %bitcast.79, bf16[64,512,256]{1,2,0:T(8,128)(2,1)} %get-tuple-element.8, bf16[64,512,256]{1,2,0:T(8,128)(2,1)} %get-tuple-element.7, bf16[64,512,256]{1,2,0:T(8,128)(2,1)} %get-tuple-element.6), kind=kOutput, calls=%fused_computation.67 | convolution fusion | flops 8858370048 | bytes 83886080 | tf_op jit(solution)/shard_map/edi,diy->dye/dot_general | solution.py:50
  1069.8 12.0 copy.65
  1087.2 12.0 copy.72
  1099.2 171.9 %all-to-all-done.3 = bf16[1,64,512,128]{3,1,0,2:T(8,128)(2,1)} async-done(((bf16[1,64,512,128]{3,1,0,2:T(8,128)(2,1)}), bf16[1,64,512,128]{3,1,0,2:T(8,128)(2,1)}, u32[]{:S(2)}, u32[]{:S(2)}) %all-to-all-start.3) | async-done | bytes 8388640 | tf_op jit(solution)/shard_map/all_to_all | solution.py:79
  1271.1 12.0 copy.71
  1283.1 13.8 %pad_maximum_fusion = bf16[2,8,64,64,128]{4,3,2,1,0:T(8,128)(2,1)} fusion(bf16[1,8,64,64,128]{4,3,2,1,0:T(8,128)(2,1)} %bitcast.85, bf16[1,8,64,64,128]{4,3,2,1,0:T(8,128)(2,1)} %bitcast.84), kind=kLoop, calls=%fused_computation.13 | loop fusion | flops 8388608 | bytes 33554432 | tf_op jit(solution)/shard_map/stack | solution.py:81
  (46 shorter events, 42.4 us)
Async XLA Ops:
  130.4 190.9 %all-to-all-start = ((bf16[32,256,1024]{2,0,1:T(8,128)(2,1)}), bf16[32,256,1024]{2,0,1:T(8,128)(2,1)}, u32[]{:S(2)}, u32[]{:S(2)}) async-start(bf16[32,256,1024]{2,0,1:T(8,128)(2,1)} %copy.49), calls=%async_computation | async-start | bytes 33554432 | tf_op jit(solution)/shard_map/all_to_all | solution.py:76
  137.6 18.7 %copy-start.5 = (s32[256]{0:T(256)S(1)}, s32[256]{0:T(256)}, u32[]{:S(2)}) copy-start(s32[256]{0:T(256)} %param.10) | copy-start | bytes 3076
  137.7 18.8 %copy-start.6 = (s32[256]{0:T(256)S(1)}, s32[256]{0:T(256)}, u32[]{:S(2)}) copy-start(s32[256]{0:T(256)} %param.11) | copy-start | bytes 3076
  156.5 414.6 %copy-start.3 = (pred[32,32]{1,0:T(8,128)(4,1)}, pred[32,32]{1,0:T(8,128)(4,1)S(1)}, u32[]{:S(2)}) copy-start(pred[32,32]{1,0:T(8,128)(4,1)S(1)} %iota_compare_fusion.2) | copy-start | bytes 3076
  156.5 414.8 %copy-start.1 = (pred[32,32]{1,0:T(8,128)(4,1)}, pred[32,32]{1,0:T(8,128)(4,1)S(1)}, u32[]{:S(2)}) copy-start(pred[32,32]{1,0:T(8,128)(4,1)S(1)} %iota_compare_fusion.1) | copy-start | bytes 3076
  321.4 375.5 %all-to-all-start.2 = ((bf16[32,256,1024]{2,0,1:T(8,128)(2,1)}), bf16[32,256,1024]{2,0,1:T(8,128)(2,1)}, u32[]{:S(2)}, u32[]{:S(2)}) async-start(bf16[32,256,1024]{2,0,1:T(8,128)(2,1)} %copy.58), calls=%async_computation.2 | async-start | bytes 33554432 | tf_op jit(solution)/shard_map/all_to_all | solution.py:76
  696.9 384.9 %all-to-all-start.1 = ((bf16[1,64,512,128]{3,1,0,2:T(8,128)(2,1)}), bf16[1,64,512,128]{3,1,0,2:T(8,128)(2,1)}, u32[]{:S(2)}, u32[]{:S(2)}) async-start(bf16[1,64,512,128]{3,1,0,2:T(8,128)(2,1)} %copy.56), calls=%async_computation.1 | async-start | bytes 16777216 | tf_op jit(solution)/shard_map/all_to_all | solution.py:79
  742.1 202.3 %copy-start.4 = (pred[32,32]{1,0:T(8,128)(4,1)S(1)}, pred[32,32]{1,0:T(8,128)(4,1)}, u32[]{:S(2)}) copy-start(pred[32,32]{1,0:T(8,128)(4,1)} %copy-done.3) | copy-start | bytes 3076
  742.1 202.5 %copy-start.2 = (pred[32,32]{1,0:T(8,128)(4,1)S(1)}, pred[32,32]{1,0:T(8,128)(4,1)}, u32[]{:S(2)}) copy-start(pred[32,32]{1,0:T(8,128)(4,1)} %copy-done.1) | copy-start | bytes 3076
  1023.5 37.1 %copy-start = (bf16[64,128,32]{1,2,0:T(8,128)(2,1)S(1)}, bf16[64,128,32]{1,2,0:T(8,128)(2,1)}, u32[]{:S(2)}) copy-start(bf16[64,128,32]{1,2,0:T(8,128)(2,1)} %fusion.21) | copy-start | bytes 1572868
  1081.8 189.3 %all-to-all-start.3 = ((bf16[1,64,512,128]{3,1,0,2:T(8,128)(2,1)}), bf16[1,64,512,128]{3,1,0,2:T(8,128)(2,1)}, u32[]{:S(2)}, u32[]{:S(2)}) async-start(bf16[1,64,512,128]{3,1,0,2:T(8,128)(2,1)} %copy.65), calls=%async_computation.3 | async-start | bytes 16777216 | tf_op jit(solution)/shard_map/all_to_all | solution.py:79
where the time goes:
time: 1310 us; the launch traced here: 1300 us
  other arithmetic  567 us (43%)
  matrix products  290 us (22%)
  waiting for transfers between devices  210 us (16%)
  local copies, waits for them, and re-layouts  204 us (16%)
  starting transfers between devices  25.5 us (2%)
    another operation x7, other arithmetic, power_step(): lower = jnp.linalg.cholesky(gram)  375 us
    all_to_all x2, waiting for transfers between devices, per_device(): lax.all_to_all(formed[None], 'chan', split_axis=2, concat_axis=0, tiled=T...  172 us
    another operation x1, other arithmetic  126 us
    dot_general x2, matrix products, power_step(): jnp.einsum('edi,diy->dye', voltage_input, steering_weight, preferred_elem...  74.1 us
    gather x1, local copies, waits for them, and re-layouts, per_device(): ordered = jnp.take(voltages, order, axis=2) * keep  61.8 us
    squeeze x3, local copies, waits for them, and re-layouts, per_device(): ordered[part]  61.6 us
    dot_general x2, matrix products, power_step(): jnp.einsum('crs,csb->crb', subspace_vectors, steering_weight, preferred_e...  60.9 us
    dot_general x2, matrix products, power_step(): jnp.einsum('nwg,wny->ngy', projected_input, voltage_input, preferred_elem...  51.2 us
  transfers between devices with their start and end apart: 4, of which 2 were waited for; matrix products, arithmetic and copies ran while one was open for 70% of the time, Pallas kernels for 0%

commit v1 on v0

--- a/solution.py
+++ b/solution.py
@@ -1,15 +1,267 @@
+import functools
 import math
 
 import jax
 import jax.numpy as jnp
+import numpy as np
 from jax import lax
+from jax.experimental import pallas as pl
+from jax.experimental.pallas import tpu as pltpu
 from jax.sharding import PartitionSpec as P
 
 CH = 2048
-SUB = 2
-
+CHUNKS = 4
+BLOCK = 8
+TILE = 16
 
 TWO_PI = 2.0 * math.pi
+NT = (((1,), (1,)), ((), ()))
+TN = (((0,), (0,)), ((), ()))
+
+
+def series(func, odd):
+    fit = np.polynomial.chebyshev.Chebyshev.interpolate(
+        lambda r: func(TWO_PI * r), 11 if odd else 10, domain=[-0.5, 0.5]
+    )
+    powers = fit.convert(kind=np.polynomial.Polynomial).coef
+    return [float(value) for value in powers[1 if odd else 0 :: 2]]
+
+
+COS = series(np.cos, False)
+SIN = series(np.sin, True)
+
+
+def evaluate(coefficients, square, factor):
+    total = coefficients[-1] * factor
+    for value in coefficients[-2::-1]:
+        total = total * square + value * factor
+    return total
+
+
+def arrange_kernel(chunks, per, place_ref, volt_ref, turn_ref, keep_ref, *rest):
+    outs, (held, sems) = rest[:chunks], rest[chunks:]
+    part, block = pl.program_id(0), pl.program_id(1)
+    blocks = pl.num_programs(1)
+    step = part * blocks + block
+    half = lax.rem(step, 2)
+    times = volt_ref.shape[1]
+
+    def drain(which):
+        for row in range(TILE):
+            pltpu.make_async_copy(
+                held.at[which, row], outs[0].at[0, 0, 0], sems.at[which, row]
+            ).wait()
+
+    @pl.when(step >= 2)
+    def _():
+        drain(half)
+
+    for start in range(0, times, TILE):
+        rows = volt_ref[0, start : start + TILE].reshape(TILE * TILE, -1)
+        turned = jnp.dot(turn_ref[...], rows, preferred_element_type=jnp.float32)
+        turned = (turned * keep_ref[...]).astype(jnp.bfloat16)
+        held[half, :, start : start + TILE, :] = turned.reshape(TILE, TILE, -1)
+    for row in range(TILE):
+        place = place_ref[block * TILE + row]
+        slots = chunks * per
+        owner, local = place // slots, lax.rem(place, slots)
+        chunk, inner = local // per, lax.rem(local, per)
+        for index in range(chunks):
+
+            @pl.when(chunk == index)
+            def _():
+                pltpu.make_async_copy(
+                    held.at[half, row], outs[index].at[owner, inner, part], sems.at[half, row]
+                ).start()
+
+    @pl.when(step == 2 * blocks - 1)
+    def _():
+        drain(1 - half)
+        drain(half)
+
+
+def arrange(voltages, place, keep, owners, slots):
+    parts, times, channels, signals = voltages.shape
+    per = slots // CHUNKS
+    row = jnp.arange(TILE * TILE)
+    turn = (row[None, :] == (row % TILE * TILE + row // TILE)[:, None]).astype(jnp.bfloat16)
+    shape = jax.ShapeDtypeStruct((owners, per, parts, times, signals), jnp.bfloat16)
+    return pl.pallas_call(
+        functools.partial(arrange_kernel, CHUNKS, per),
+        grid_spec=pltpu.PrefetchScalarGridSpec(
+            num_scalar_prefetch=1,
+            grid=(parts, channels // TILE),
+            in_specs=[
+                pl.BlockSpec((1, times, TILE, signals), lambda s, c, _: (s, 0, c, 0)),
+                pl.BlockSpec((TILE * TILE, TILE * TILE), lambda s, c, _: (0, 0)),
+                pl.BlockSpec((1, signals), lambda s, c, _: (0, 0)),
+            ],
+            out_specs=[pl.BlockSpec(memory_space=pl.ANY)] * CHUNKS,
+            scratch_shapes=[
+                pltpu.VMEM((2, TILE, times, signals), jnp.bfloat16),
+                pltpu.SemaphoreType.DMA((2, TILE)),
+            ],
+        ),
+        out_shape=[shape] * CHUNKS,
+        compiler_params=pltpu.CompilerParams(vmem_limit_bytes=40 * 2**20),
+        cost_estimate=pl.CostEstimate(
+            flops=2 * TILE * TILE * voltages.size, bytes_accessed=4 * voltages.size, transcendentals=0
+        ),
+        name="arrange",
+    )(place, voltages, turn, keep)
+
+
+def invert_factor(gram):
+    count, rank = gram.shape[0], gram.shape[1]
+    row_no = lax.broadcasted_iota(jnp.int32, (count, rank, rank), 1)
+    col_no = lax.broadcasted_iota(jnp.int32, (count, rank, rank), 2)
+    inverse = jnp.where(row_no == col_no, 1.0, 0.0)
+    for j in range(rank):
+        scale = 1.0 / jnp.sqrt(gram[:, j : j + 1, j : j + 1])
+        under = jnp.where(row_no > j, gram[:, :, j : j + 1] * scale, 0.0)
+        upper_row = gram[:, j : j + 1, :] * scale
+        inverse_row = inverse[:, j : j + 1, :] * scale
+        gram = gram - under * upper_row
+        inverse = jnp.where(row_no == j, inverse_row, inverse - under * inverse_row)
+    return inverse
+
+
+def beam_kernel(freq_ref, x_ref, state_ref, delay_ref, out_ref, track_ref, image, gram, weight, clean):
+    block, parts = x_ref.shape[1], x_ref.shape[2]
+    signals = x_ref.shape[-1]
+    beams, stations = delay_ref.shape
+    owners, beam_rows = out_ref.shape[0], out_ref.shape[3]
+    highest = lax.Precision.HIGHEST
+    base = pl.program_id(0) * block
+
+    def samples(i, part):
+        return x_ref[:, i, part].reshape(-1, signals)
+
+    track_ref[...] = state_ref[...]
+    for part in range(parts):
+        for i in range(block):
+            x = samples(i, part)
+            state = track_ref[i]
+            y = lax.dot_general(
+                state.astype(jnp.bfloat16), x, NT, preferred_element_type=jnp.float32
+            ).astype(jnp.bfloat16)
+            z = jnp.dot(y, x, preferred_element_type=jnp.float32) + x.shape[0] * state
+            image[i] = z
+            gram[i] = lax.dot_general(
+                z, z, NT, precision=highest, preferred_element_type=jnp.float32
+            )
+        inverse = invert_factor(gram[...])
+        for i in range(block):
+            x = samples(i, part)
+            state = jnp.dot(
+                inverse[i], image[i], precision=highest, preferred_element_type=jnp.float32
+            )
+            track_ref[i] = state
+            rows = state.astype(jnp.bfloat16)
+            p = lax.dot_general(rows, x, NT, preferred_element_type=jnp.float32)
+            lost = lax.dot_general(
+                p.astype(jnp.bfloat16), rows, TN, preferred_element_type=jnp.float32
+            )
+            times = x.shape[0]
+            clean[i, part * times : (part + 1) * times, :] = (
+                x.astype(jnp.float32) - lost
+            ).astype(jnp.bfloat16)
+
+    factor = 1.0 / math.sqrt(stations)
+
+    def form(i, carry):
+        turns = delay_ref[...] * freq_ref[base + i]
+        turns = turns - jnp.round(turns)
+        square = turns * turns
+        re = evaluate(COS, square, factor).astype(jnp.bfloat16)
+        im = evaluate(SIN, square, factor) * turns
+        weight[:beams, :stations] = re
+        weight[:beams, stations:] = (-im).astype(jnp.bfloat16)
+        weight[beams:, :stations] = im.astype(jnp.bfloat16)
+        weight[beams:, stations:] = re
+        formed = lax.dot_general(
+            weight[...], clean[i], NT, preferred_element_type=jnp.float32
+        ).astype(jnp.bfloat16)
+        times = formed.shape[1] // parts
+        for part in range(parts):
+            out_ref[:, part, i] = formed[:, part * times : (part + 1) * times].reshape(
+                owners, beam_rows, times
+            )
+        return carry
+
+    lax.fori_loop(0, block, form, 0)
+
+
+def form_beams(x, state, freq, delays, owners):
+    sources, slots, parts, times, signals = x.shape
+    rank = state.shape[1]
+    beams, stations = delays.shape
+    total = sources * times
+    rows = 2 * beams // owners
+    return pl.pallas_call(
+        beam_kernel,
+        grid=(slots // BLOCK,),
+        in_specs=[
+            pl.BlockSpec(memory_space=pltpu.SMEM),
+            pl.BlockSpec((sources, BLOCK, parts, times, signals), lambda b: (0, b, 0, 0, 0)),
+            pl.BlockSpec((BLOCK, rank, signals), lambda b: (b, 0, 0)),
+            pl.BlockSpec((beams, stations), lambda b: (0, 0)),
+        ],
+        out_specs=[
+            pl.BlockSpec((owners, parts, BLOCK, rows, total), lambda b: (0, 0, b, 0, 0)),
+            pl.BlockSpec((BLOCK, rank, signals), lambda b: (b, 0, 0)),
+        ],
+        out_shape=[
+            jax.ShapeDtypeStruct((owners, parts, slots, rows, total), jnp.bfloat16),
+            jax.ShapeDtypeStruct(state.shape, jnp.float32),
+        ],
+        scratch_shapes=[
+            pltpu.VMEM((BLOCK, rank, signals), jnp.float32),
+            pltpu.VMEM((BLOCK, rank, rank), jnp.float32),
+            pltpu.VMEM((2 * beams, 2 * stations), jnp.bfloat16),
+            pltpu.VMEM((BLOCK, parts * total, signals), jnp.bfloat16),
+        ],
+        compiler_params=pltpu.CompilerParams(vmem_limit_bytes=48 * 2**20),
+        cost_estimate=pl.CostEstimate(
+            flops=slots * parts * 2 * total * signals * (2 * beams + 6 * rank) * 4,
+            bytes_accessed=2 * x.size + 8 * state.size + 4 * slots * parts * beams * total,
+            transcendentals=0,
+        ),
+        name="form_beams",
+    )(freq, x, state, delays)
+
+
+def per_device_blocks(voltages, subspace, order, beam_seeds, flagged, owners, groups):
+    signals = voltages.shape[-1]
+    stations = signals // 2
+    slots = subspace.shape[1]
+    per_group = order.shape[0]
+    per = slots // CHUNKS
+    marks = jnp.any(flagged[:, None] == jnp.arange(stations, dtype=jnp.int32)[None, :], axis=0)
+    keep = jnp.where(marks, 0.0, 1.0).astype(jnp.float32)
+    keep = jnp.concatenate([keep, keep])[None, :]
+    slot_no = jnp.arange(per_group, dtype=jnp.int32)
+    match = order[None, :] == slot_no[:, None]
+    place = jnp.sum(jnp.where(match, slot_no[None, :], 0), axis=1).astype(jnp.int32)
+    pieces = arrange(voltages, place, keep, owners, slots)
+
+    group = lax.axis_index("chan")
+    chosen = lax.dynamic_slice_in_dim(order, lax.axis_index("tm") * slots, slots)
+    freq = 1.0 + (group * per_group + chosen).astype(jnp.float32) / CH
+    station_no = jnp.arange(stations, dtype=jnp.int32) + 1
+    delays = (beam_seeds[:, None] * station_no[None, :] % 65521).astype(jnp.float32) / 65521.0
+
+    formed_all, tracked = [], []
+    for chunk in range(CHUNKS):
+        x = lax.all_to_all(pieces[chunk], "tm", split_axis=0, concat_axis=0, tiled=True)
+        first = chunk * per
+        formed, state = form_beams(
+            x, subspace[0, first : first + per], freq[first : first + per], delays, groups
+        )
+        tracked.append(state)
+        formed_all.append(lax.all_to_all(formed, "chan", split_axis=0, concat_axis=0, tiled=True))
+    beams = jnp.concatenate(formed_all, axis=2)
+    return jnp.swapaxes(beams, 0, 1), jnp.concatenate(tracked)[None]
 
 
 def beam_weights(beam_seeds, channels, stations, total_channels):
@@ -56,7 +308,7 @@
     return (tracked, beams.astype(jnp.bfloat16))
 
 
-def per_device(voltages, subspace, order, beam_seeds, flagged):
+def per_device_plain(voltages, subspace, order, beam_seeds, flagged):
     signals = voltages.shape[-1]
     stations = signals // 2
     slots = subspace.shape[1]
@@ -72,7 +324,7 @@
     steering_weight = beam_weights(beam_seeds, channels, stations, CH)
     state = subspace[0]
     results = []
-    for part in range(SUB):
+    for part in range(voltages.shape[0]):
         turned = lax.all_to_all(ordered[part], "tm", split_axis=1, concat_axis=0, tiled=True)
         state, formed = power_step(turned, state, steering_weight)
         results.append(
@@ -83,6 +335,22 @@
 
 
 def solution(mesh):
+    owners, groups = mesh.shape["tm"], mesh.shape["chan"]
+
+    def per_device(voltages, subspace, order, beam_seeds, flagged):
+        times, channels = voltages.shape[1], voltages.shape[2]
+        whole = (
+            times % TILE == 0
+            and channels % TILE == 0
+            and subspace.shape[1] % (CHUNKS * BLOCK) == 0
+            and 2 * beam_seeds.shape[0] % (groups * TILE) == 0
+        )
+        if whole:
+            return per_device_blocks(
+                voltages, subspace, order, beam_seeds, flagged, owners, groups
+            )
+        return per_device_plain(voltages, subspace, order, beam_seeds, flagged)
+
     return jax.shard_map(
         per_device,
         mesh=mesh,

time: 1310 us -> 844 us (0.64)
  other arithmetic: 567 us -> 16.1 us
  matrix products: 290 us -> 0 us
  blocking collectives: 0 us -> 290 us
  Pallas kernels: 0 us -> 284 us
  local copies, waits for them, and re-layouts: 204 us -> 22.3 us
    another operation x14 -> x0, other arithmetic: 541 us -> none  [the longest x7 375 us: power_step(): lower = jnp.linalg.cholesky(gram)]
    all_to_all x0 -> x3, blocking collectives: none -> 290 us  [per_device_blocks(): lax.all_to_all(pieces[chunk], 'tm', split_axis=0, concat_axis=0, tiled=True)]
    pallas_call x0 -> x5, Pallas kernels: none -> 284 us  [the longest x4 241 us: form_beams(): pl.pallas_call(beam_kernel, grid=(slots // BLOCK,), in_specs=[pl.BlockSpe...]
    dot_general x12 -> x0, matrix products: 255 us -> none  [the longest x2 74.1 us: power_step(): jnp.einsum('edi,diy->dye', voltage_input, steering_weight, preferred_elem...]
    gather x1 -> x0, local copies, waits for them, and re-layouts: 61.8 us -> none  [per_device(): ordered = jnp.take(voltages, order, axis=2) * keep]
    squeeze x3 -> x1, local copies, waits for them, and re-layouts: 61.6 us -> 6.73 us  [per_device_blocks(): subspace[0, first:first + per]]
    all_to_all x4 -> x0, local copies, waits for them, and re-layouts: 52.6 us -> none  [the longest x2 28.5 us: per_device(): lax.all_to_all(ordered[part], 'tm', split_axis=1, concat_axis=0, tiled=True)]
    another operation x2 -> x0, matrix products: 34.9 us -> none  [power_step(): tracked = jax.scipy.linalg.solve_triangular(lower, beam_image, lower=True)]
  transfers between devices with their start and end apart: 4 -> 5, of which waited for: 2 -> 5; matrix products, arithmetic and copies ran while one was open for 70% -> 2% of each run, Pallas kernels for 0% -> 29%
where the time goes in v1:
time: 844 us; the launch traced here: 840 us
  blocking collectives  290 us (34%)
  Pallas kernels  284 us (34%)
  waiting for transfers between devices  202 us (24%)
  starting transfers between devices  24.1 us (3%)
  local copies, waits for them, and re-layouts  22.3 us (3%)
  other arithmetic  16.1 us (2%)
    all_to_all x3, blocking collectives, per_device_blocks(): lax.all_to_all(pieces[chunk], 'tm', split_axis=0, concat_axis=0, tiled=True)  290 us
    pallas_call x4, Pallas kernels, form_beams(): pl.pallas_call(beam_kernel, grid=(slots // BLOCK,), in_specs=[pl.BlockSpe...  241 us
    all_to_all x4, waiting for transfers between devices, per_device_blocks(): lax.all_to_all(formed, 'chan', split_axis=0, concat_axis=0, tiled=True)  181 us
    pallas_call x1, Pallas kernels, arrange(): pl.pallas_call(functools.partial(arrange_kernel, CHUNKS, per), grid_spec=...  43.6 us
    all_to_all x1, waiting for transfers between devices, per_device_blocks(): lax.all_to_all(pieces[chunk], 'tm', split_axis=0, concat_axis=0, tiled=True)  21.5 us
    all_to_all x4, starting transfers between devices, per_device_blocks(): lax.all_to_all(formed, 'chan', split_axis=0, concat_axis=0, tiled=True)  18.4 us
  transfers between devices with their start and end apart: 5, of which 5 were waited for; matrix products, arithmetic and copies ran while one was open for 2% of the time, Pallas kernels for 29%

profile of v1, /device:TPU:0, one launch (start us, length us, event | category | flops | bytes accessed | tf_op | source)
XLA Modules:
  0.0 839.8 jit_solution(4133267404826971196)
XLA Ops:
  0.6 0.1 fusion.5.turn_ref
  0.7 0.7 fusion.6
  1.5 0.8 select_reduce_fusion.place_ref
  2.3 43.6 %arrange.1 = (bf16[4,16,2,32,1024]{4,3,2,1,0:T(8,128)(2,1)S(1)}, bf16[4,16,2,32,1024]{4,3,2,1,0:T(8,128)(2,1)}, bf16[4,16,2,32,1024]{4,3,2,1,0:T(8,128)(2,1)}, bf16[4,16,2,32,1024]{4,3,2,1,0:T(8,128)(2,1)}) custom-call(s32[256]{0:T(256)S(1)} %select_reduce_fusion.place_ref, bf16[2,32,256,1024]{3,2,1,0:T(8,128)(2,1)} %volt_ref.1, ...), custom_call_target="tpu_custom_call" | custom-call | flops 8589934592 | bytes 67108864 | tf_op jit(solution)/shard_map/arrange/pallas_call | solution.py:89
  45.9 98.7 %all_to_all.40.x_ref = bf16[4,16,2,32,1024]{4,3,2,1,0:T(8,128)(2,1)} all-to-all(bf16[4,16,2,32,1024]{4,3,2,1,0:T(8,128)(2,1)S(1)} %get-tuple-element.14), channel_id=1, replica_groups=mesh['tm'=4,'chan'=8] {'tm'}, dimensions={0} | all-to-all | bytes 16777216 | tf_op jit(solution)/shard_map/all_to_all | solution.py:256
  144.6 96.2 %all_to_all.41.x_ref = bf16[4,16,2,32,1024]{4,3,2,1,0:T(8,128)(2,1)} all-to-all(bf16[4,16,2,32,1024]{4,3,2,1,0:T(8,128)(2,1)S(1)} %copy-done.6), channel_id=1, replica_groups=mesh['tm'=4,'chan'=8] {'tm'}, dimensions={0} | all-to-all | bytes 16777216 | tf_op jit(solution)/shard_map/all_to_all | solution.py:256
  240.8 94.7 %all_to_all.42.x_ref = bf16[4,16,2,32,1024]{4,3,2,1,0:T(8,128)(2,1)} all-to-all(bf16[4,16,2,32,1024]{4,3,2,1,0:T(8,128)(2,1)S(1)} %bitcast.15), channel_id=1, replica_groups=mesh['tm'=4,'chan'=8] {'tm'}, dimensions={0} | all-to-all | bytes 16777216 | tf_op jit(solution)/shard_map/all_to_all | solution.py:256
  335.5 5.8 all-to-all-start.6
  341.5 0.4 fusion.1.delay_ref
  341.8 6.7 slice_bitcast_fusion.3
  348.6 60.2 %form_beams.4 = (bf16[8,2,16,64,128]{4,3,2,1,0:T(8,128)(2,1)}, f32[16,32,1024]{2,1,0:T(8,128)S(1)}) custom-call(f32[16]{0:T(128)S(1)} %get-tuple-element.34.freq_ref, bf16[4,16,2,32,1024]{4,3,2,1,0:T(8,128)(2,1)} %all_to_all.40.x_ref, f32[16,32,1024]{2,1,0:T(8,128)S(1)} %get-tuple-element.30.state_ref, f32[256,512]{1,0:T(8,128)S(1)} %fusion.1.delay_ref), custom_call_target="tpu_custom_call" | custom-call | flops 23622320128 | bytes 16777216 | tf_op jit(solution)/shard_map/form_beams/pallas_call | solution.py:201
  408.7 21.5 %all-to-all-done.6.x_ref = bf16[4,16,2,32,1024]{4,3,2,1,0:T(8,128)(2,1)} async-done(((bf16[4,16,2,32,1024]{4,3,2,1,0:T(8,128)(2,1)}), bf16[4,16,2,32,1024]{4,3,2,1,0:T(8,128)(2,1)}, u32[]{:S(2)}, u32[]{:S(2)}) %all-to-all-start.6) | async-done | bytes 8388640 | tf_op jit(solution)/shard_map/all_to_all | solution.py:256
  430.2 4.6 all-to-all-start.1
  434.8 1.6 copy-done.4
  436.4 60.4 %form_beams.5 = (bf16[8,2,16,64,128]{4,3,2,1,0:T(8,128)(2,1)}, f32[16,32,1024]{2,1,0:T(8,128)S(1)}) custom-call(f32[16]{0:T(128)S(1)} %get-tuple-element.37.freq_ref, bf16[4,16,2,32,1024]{4,3,2,1,0:T(8,128)(2,1)} %all_to_all.41.x_ref, f32[16,32,1024]{2,1,0:T(8,128)S(1)} %copy-done.4, f32[256,512]{1,0:T(8,128)S(1)} %fusion.1.delay_ref), custom_call_target="tpu_custom_call" | custom-call | flops 23622320128 | bytes 16777216 | tf_op jit(solution)/shard_map/form_beams/pallas_call | solution.py:201
  496.8 1.4 copy-done.1
  498.2 30.6 %all-to-all-done.1 = bf16[8,2,16,64,128]{4,3,2,1,0:T(8,128)(2,1)} async-done(((bf16[8,2,16,64,128]{4,3,2,1,0:T(8,128)(2,1)}), bf16[8,2,16,64,128]{4,3,2,1,0:T(8,128)(2,1)}, u32[]{:S(2)}, u32[]{:S(2)}) %all-to-all-start.1) | async-done | bytes 4194336 | tf_op jit(solution)/shard_map/all_to_all | solution.py:262
  528.8 4.6 all-to-all-start.3
  533.4 1.6 copy-done.2
  535.0 60.2 %form_beams.6 = (bf16[8,2,16,64,128]{4,3,2,1,0:T(8,128)(2,1)}, f32[16,32,1024]{2,1,0:T(8,128)S(1)}) custom-call(f32[16]{0:T(128)S(1)} %get-tuple-element.36.freq_ref, bf16[4,16,2,32,1024]{4,3,2,1,0:T(8,128)(2,1)} %all_to_all.42.x_ref, f32[16,32,1024]{2,1,0:T(8,128)S(1)} %copy-done.2, f32[256,512]{1,0:T(8,128)S(1)} %fusion.1.delay_ref), custom_call_target="tpu_custom_call" | custom-call | flops 23622320128 | bytes 16777216 | tf_op jit(solution)/shard_map/form_beams/pallas_call | solution.py:201
  595.1 1.3 copy-done.3
  596.5 30.9 %all-to-all-done.3 = bf16[8,2,16,64,128]{4,3,2,1,0:T(8,128)(2,1)} async-done(((bf16[8,2,16,64,128]{4,3,2,1,0:T(8,128)(2,1)}), bf16[8,2,16,64,128]{4,3,2,1,0:T(8,128)(2,1)}, u32[]{:S(2)}, u32[]{:S(2)}) %all-to-all-start.3) | async-done | bytes 4194336 | tf_op jit(solution)/shard_map/all_to_all | solution.py:262
  627.4 4.6 all-to-all-start.5
  632.0 1.6 copy-done
  633.6 60.2 %form_beams.7 = (bf16[8,2,16,64,128]{4,3,2,1,0:T(8,128)(2,1)}, f32[16,32,1024]{2,1,0:T(8,128)S(1)}) custom-call(f32[16]{0:T(128)S(1)} %get-tuple-element.35.freq_ref, bf16[4,16,2,32,1024]{4,3,2,1,0:T(8,128)(2,1)} %all-to-all-done.6.x_ref, f32[16,32,1024]{2,1,0:T(8,128)S(1)} %copy-done, f32[256,512]{1,0:T(8,128)S(1)} %fusion.1.delay_ref), custom_call_target="tpu_custom_call" | custom-call | flops 23622320128 | bytes 16777216 | tf_op jit(solution)/shard_map/form_beams/pallas_call | solution.py:201
  693.8 1.3 copy-done.5
  695.1 30.9 %all-to-all-done.5 = bf16[8,2,16,64,128]{4,3,2,1,0:T(8,128)(2,1)} async-done(((bf16[8,2,16,64,128]{4,3,2,1,0:T(8,128)(2,1)}), bf16[8,2,16,64,128]{4,3,2,1,0:T(8,128)(2,1)}, u32[]{:S(2)}, u32[]{:S(2)}) %all-to-all-start.5) | async-done | bytes 4194336 | tf_op jit(solution)/shard_map/all_to_all | solution.py:262
  726.0 4.6 all-to-all-start.7
  730.6 5.8 maximum_bitcast_fusion.1
  736.4 88.2 %all-to-all-done.7 = bf16[8,2,16,64,128]{4,3,2,1,0:T(8,128)(2,1)} async-done(((bf16[8,2,16,64,128]{4,3,2,1,0:T(8,128)(2,1)}), bf16[8,2,16,64,128]{4,3,2,1,0:T(8,128)(2,1)}, u32[]{:S(2)}, u32[]{:S(2)}) %all-to-all-start.7) | async-done | bytes 4194336 | tf_op jit(solution)/shard_map/all_to_all | solution.py:262
  824.6 8.2 maximum_bitcast_fusion
  832.9 6.7 copy.8
  (23 shorter events, 0.2 us)
Async XLA Ops:
  45.9 98.7 %copy-start.6 = (bf16[4,16,2,32,1024]{4,3,2,1,0:T(8,128)(2,1)S(1)}, bf16[4,16,2,32,1024]{4,3,2,1,0:T(8,128)(2,1)}, u32[]{:S(2)}) copy-start(bf16[4,16,2,32,1024]{4,3,2,1,0:T(8,128)(2,1)} %get-tuple-element.16) | copy-start | bytes 25165828
  45.9 194.9 %slice-start = ((s8[8388608]{0:T(1024)(128)(4,1)}), s8[4194304]{0:T(1024)(128)(4,1)S(1)}, s32[]{:S(2)}) async-start(s8[8388608]{0:T(1024)(128)(4,1)} %bitcast.14), calls=%async_computation.8 | async-start | bytes 8388608
  144.6 96.2 %slice-start.1 = ((s8[8388608]{0:T(1024)(128)(4,1)}), s8[4194304]{0:T(1024)(128)(4,1)S(1)}, s32[]{:S(2)}) async-start(s8[8388608]{0:T(1024)(128)(4,1)} %bitcast.14), calls=%async_computation.9 | async-start | bytes 8388608
  335.5 5.8 copy-start.7
  335.5 6.0 copy-start.8
  335.5 94.7 %all-to-all-start.6 = ((bf16[4,16,2,32,1024]{4,3,2,1,0:T(8,128)(2,1)}), bf16[4,16,2,32,1024]{4,3,2,1,0:T(8,128)(2,1)}, u32[]{:S(2)}, u32[]{:S(2)}) async-start(bf16[4,16,2,32,1024]{4,3,2,1,0:T(8,128)(2,1)} %get-tuple-element.20), calls=%async_computation.6 | async-start | bytes 16777216 | tf_op jit(solution)/shard_map/all_to_all | solution.py:256
  430.2 98.6 %all-to-all-start.1 = ((bf16[8,2,16,64,128]{4,3,2,1,0:T(8,128)(2,1)}), bf16[8,2,16,64,128]{4,3,2,1,0:T(8,128)(2,1)}, u32[]{:S(2)}, u32[]{:S(2)}) async-start(bf16[8,2,16,64,128]{4,3,2,1,0:T(8,128)(2,1)} %get-tuple-element.15), calls=%async_computation.1 | async-start | bytes 8388608 | tf_op jit(solution)/shard_map/all_to_all | solution.py:262
  434.8 1.6 copy-start.4
  496.8 1.4 copy-start.1
  528.8 98.6 %all-to-all-start.3 = ((bf16[8,2,16,64,128]{4,3,2,1,0:T(8,128)(2,1)}), bf16[8,2,16,64,128]{4,3,2,1,0:T(8,128)(2,1)}, u32[]{:S(2)}, u32[]{:S(2)}) async-start(bf16[8,2,16,64,128]{4,3,2,1,0:T(8,128)(2,1)} %get-tuple-element.17), calls=%async_computation.3 | async-start | bytes 8388608 | tf_op jit(solution)/shard_map/all_to_all | solution.py:262
  533.4 1.6 copy-start.2
  595.1 1.4 copy-start.3
  627.4 98.6 %all-to-all-start.5 = ((bf16[8,2,16,64,128]{4,3,2,1,0:T(8,128)(2,1)}), bf16[8,2,16,64,128]{4,3,2,1,0:T(8,128)(2,1)}, u32[]{:S(2)}, u32[]{:S(2)}) async-start(bf16[8,2,16,64,128]{4,3,2,1,0:T(8,128)(2,1)} %get-tuple-element.19), calls=%async_computation.5 | async-start | bytes 8388608 | tf_op jit(solution)/shard_map/all_to_all | solution.py:262
  632.0 1.6 copy-start
  693.8 1.3 copy-start.5
  726.0 98.6 %all-to-all-start.7 = ((bf16[8,2,16,64,128]{4,3,2,1,0:T(8,128)(2,1)}), bf16[8,2,16,64,128]{4,3,2,1,0:T(8,128)(2,1)}, u32[]{:S(2)}, u32[]{:S(2)}) async-start(bf16[8,2,16,64,128]{4,3,2,1,0:T(8,128)(2,1)} %get-tuple-element.21), calls=%async_computation.7 | async-start | bytes 8388608 | tf_op jit(solution)/shard_map/all_to_all | solution.py:262

commit v2 on v1

--- a/solution.py
+++ b/solution.py
@@ -10,7 +10,7 @@
 from jax.sharding import PartitionSpec as P
 
 CH = 2048
-CHUNKS = 4
+CHUNKS = 8
 BLOCK = 8
 TILE = 16
 
@@ -126,9 +126,13 @@
     return inverse
 
 
-def beam_kernel(freq_ref, x_ref, state_ref, delay_ref, out_ref, track_ref, image, gram, weight, clean):
+def beam_kernel(count, freq_ref, source_ref, *rest):
+    arrived, rest = rest[:count], rest[count:]
+    state_ref, delay_ref, out_ref, track_ref, image, gram, weight, clean, x_ref = rest
     block, parts = x_ref.shape[1], x_ref.shape[2]
     signals = x_ref.shape[-1]
+    for index in range(count):
+        x_ref[source_ref[index]] = arrived[index][...]
     beams, stations = delay_ref.shape
     owners, beam_rows = out_ref.shape[0], out_ref.shape[3]
     highest = lax.Precision.HIGHEST
@@ -192,18 +196,20 @@
     lax.fori_loop(0, block, form, 0)
 
 
-def form_beams(x, state, freq, delays, owners):
-    sources, slots, parts, times, signals = x.shape
+def form_beams(pieces, source_no, state, freq, delays, owners):
+    sources = len(pieces)
+    slots, parts, times, signals = pieces[0].shape
     rank = state.shape[1]
     beams, stations = delays.shape
     total = sources * times
     rows = 2 * beams // owners
     return pl.pallas_call(
-        beam_kernel,
+        functools.partial(beam_kernel, sources),
         grid=(slots // BLOCK,),
         in_specs=[
             pl.BlockSpec(memory_space=pltpu.SMEM),
-            pl.BlockSpec((sources, BLOCK, parts, times, signals), lambda b: (0, b, 0, 0, 0)),
+            pl.BlockSpec(memory_space=pltpu.SMEM),
+            *[pl.BlockSpec((BLOCK, parts, times, signals), lambda b: (b, 0, 0, 0))] * sources,
             pl.BlockSpec((BLOCK, rank, signals), lambda b: (b, 0, 0)),
             pl.BlockSpec((beams, stations), lambda b: (0, 0)),
         ],
@@ -220,15 +226,16 @@
             pltpu.VMEM((BLOCK, rank, rank), jnp.float32),
             pltpu.VMEM((2 * beams, 2 * stations), jnp.bfloat16),
             pltpu.VMEM((BLOCK, parts * total, signals), jnp.bfloat16),
+            pltpu.VMEM((sources, BLOCK, parts, times, signals), jnp.bfloat16),
         ],
         compiler_params=pltpu.CompilerParams(vmem_limit_bytes=48 * 2**20),
         cost_estimate=pl.CostEstimate(
             flops=slots * parts * 2 * total * signals * (2 * beams + 6 * rank) * 4,
-            bytes_accessed=2 * x.size + 8 * state.size + 4 * slots * parts * beams * total,
+            bytes_accessed=2 * sources * pieces[0].size + 8 * state.size + 4 * slots * parts * beams * total,
             transcendentals=0,
         ),
         name="form_beams",
-    )(freq, x, state, delays)
+    )(freq, source_no, *pieces, state, delays)
 
 
 def per_device_blocks(voltages, subspace, order, beam_seeds, flagged, owners, groups):
@@ -251,15 +258,36 @@
     station_no = jnp.arange(stations, dtype=jnp.int32) + 1
     delays = (beam_seeds[:, None] * station_no[None, :] % 65521).astype(jnp.float32) / 65521.0
 
-    formed_all, tracked = [], []
-    for chunk in range(CHUNKS):
-        x = lax.all_to_all(pieces[chunk], "tm", split_axis=0, concat_axis=0, tiled=True)
+    me = lax.axis_index("tm")
+    source_no = jnp.bitwise_xor(me, jnp.arange(owners, dtype=jnp.int32)).astype(jnp.int32)
+    formed_all, tracked, arrived = [], [], None
+
+    def form_chunk(chunk, arrived):
         first = chunk * per
         formed, state = form_beams(
-            x, subspace[0, first : first + per], freq[first : first + per], delays, groups
+            arrived,
+            source_no,
+            subspace[0, first : first + per],
+            freq[first : first + per],
+            delays,
+            groups,
         )
         tracked.append(state)
         formed_all.append(lax.all_to_all(formed, "chan", split_axis=0, concat_axis=0, tiled=True))
+
+    for chunk in range(CHUNKS):
+        sent = [
+            lax.dynamic_index_in_dim(pieces[chunk], source_no[j], 0, keepdims=False)
+            for j in range(owners)
+        ]
+        if arrived is not None:
+            sent, arrived = lax.optimization_barrier((sent, arrived))
+            form_chunk(chunk - 1, arrived)
+        arrived = [sent[0]] + [
+            lax.ppermute(sent[j], "tm", [(i, i ^ j) for i in range(owners)])
+            for j in range(1, owners)
+        ]
+    form_chunk(CHUNKS - 1, arrived)
     beams = jnp.concatenate(formed_all, axis=2)
     return jnp.swapaxes(beams, 0, 1), jnp.concatenate(tracked)[None]
 
@@ -340,7 +368,8 @@
     def per_device(voltages, subspace, order, beam_seeds, flagged):
         times, channels = voltages.shape[1], voltages.shape[2]
         whole = (
-            times % TILE == 0
+            owners & (owners - 1) == 0
+            and times % TILE == 0
             and channels % TILE == 0
             and subspace.shape[1] % (CHUNKS * BLOCK) == 0
             and 2 * beam_seeds.shape[0] % (groups * TILE) == 0

time: 844 us -> 848 us (level); the launches traced: 840 us -> 831 us
  blocking collectives: 290 us -> 0 us
  waiting for transfers between devices: 202 us -> 347 us
  local copies, waits for them, and re-layouts: 22.3 us -> 98.5 us
  starting transfers between devices: 24.1 us -> 67.5 us
  Pallas kernels: 284 us -> 307 us
  other arithmetic: 16.1 us -> 2.12 us
    ppermute x0 -> x24, waiting for transfers between devices: none -> 328 us  [per_device_blocks(): lax.ppermute(sent[j], 'tm', [(i, i ^ j) for i in range(owners)])]
    all_to_all x3 -> x0, blocking collectives: 290 us -> none  [per_device_blocks(): lax.all_to_all(pieces[chunk], 'tm', split_axis=0, concat_axis=0, tiled=True)]
    all_to_all x5 -> x8, waiting for transfers between devices: 202 us -> 19.2 us  [form_chunk(): lax.all_to_all(formed, 'chan', split_axis=0, concat_axis=0, tiled=True)]
    unnamed x23 -> x65, local copies, waits for them, and re-layouts: 15.5 us -> 56.6 us
    squeeze x1 -> x9, local copies, waits for them, and re-layouts: 6.73 us -> 37.7 us  [the longest x8 30.6 us: per_device_blocks(): lax.dynamic_index_in_dim(pieces[chunk], source_no[j], 0, keepdims=False)]
    ppermute x0 -> x24, starting transfers between devices: none -> 28.9 us  [per_device_blocks(): lax.ppermute(sent[j], 'tm', [(i, i ^ j) for i in range(owners)])]
    all_to_all x5 -> x8, starting transfers between devices: 24.1 us -> 38.6 us  [form_chunk(): lax.all_to_all(formed, 'chan', split_axis=0, concat_axis=0, tiled=True)]
    pallas_call x1, Pallas kernels: 43.6 us -> 55.1 us  [arrange(): pl.pallas_call(functools.partial(arrange_kernel, CHUNKS, per), grid_spec=...]
  transfers between devices with their start and end apart: 5 -> 32, of which waited for: 5 -> 21; matrix products, arithmetic and copies ran while one was open for 2% -> 8% of each run, Pallas kernels for 29% -> 26%
where the time goes in v2:
time: 848 us; the launch traced here: 831 us
  waiting for transfers between devices  347 us (41%)
  Pallas kernels  307 us (36%)
  local copies, waits for them, and re-layouts  98.5 us (12%)
  starting transfers between devices  67.5 us (8%)
  between operations  8.78 us (1%)
    ppermute x24, waiting for transfers between devices, per_device_blocks(): lax.ppermute(sent[j], 'tm', [(i, i ^ j) for i in range(owners)])  328 us
    pallas_call x8, Pallas kernels, form_beams(): pl.pallas_call(functools.partial(beam_kernel, sources), grid=(slots // BL...  252 us
    unnamed x65, local copies, waits for them, and re-layouts  56.6 us
    pallas_call x1, Pallas kernels, arrange(): pl.pallas_call(functools.partial(arrange_kernel, CHUNKS, per), grid_spec=...  55.1 us
    all_to_all x8, starting transfers between devices, form_chunk(): lax.all_to_all(formed, 'chan', split_axis=0, concat_axis=0, tiled=True)  38.6 us
    squeeze x8, local copies, waits for them, and re-layouts, per_device_blocks(): lax.dynamic_index_in_dim(pieces[chunk], source_no[j], 0, keepdims=False)  30.6 us
    ppermute x24, starting transfers between devices, per_device_blocks(): lax.ppermute(sent[j], 'tm', [(i, i ^ j) for i in range(owners)])  28.9 us
    all_to_all x8, waiting for transfers between devices, form_chunk(): lax.all_to_all(formed, 'chan', split_axis=0, concat_axis=0, tiled=True)  19.2 us
  transfers between devices with their start and end apart: 32, of which 21 were waited for; matrix products, arithmetic and copies ran while one was open for 8% of the time, Pallas kernels for 26%

profile of v2, /device:TPU:0, one launch (start us, length us, event | category | flops | bytes accessed | tf_op | source)
XLA Modules:
  0.0 831.4 jit_solution(3954179600095714832)
XLA Ops:
  10.6 55.1 %arrange.1 = (bf16[4,8,2,32,1024]{4,3,2,1,0:T(8,128)(2,1)S(1)}, bf16[4,8,2,32,1024]{4,3,2,1,0:T(8,128)(2,1)S(1)}, bf16[4,8,2,32,1024]{4,3,2,1,0:T(8,128)(2,1)S(1...) custom-call(s32[256]{0:T(256)S(1)} %select_reduce_fusion.place_ref, ...), custom_call_target="tpu_custom_call" | custom-call | flops 8589934592 | bytes 67108864 | tf_op jit(solution)/shard_map/arrange/pallas_call | solution.py:89
  80.6 7.1 slice_bitcast_fusion
  87.8 12.0 %collective-permute-done.2.rest_3_ = bf16[8,2,32,1024]{3,2,1,0:T(8,128)(2,1)} collective-permute-done((bf16[8,2,32,1024]{3,2,1,0:T(8,128)(2,1)}, bf16[8,2,32,1024]{3,2,1,0:T(8,128)(2,1)}, u32[]{:S(2)}, u32[]{:S(2)}) %collective-permute-start.2) | collective-permute-done | bytes 1048608 | tf_op jit(solution)/shard_map/ppermute | solution.py:287
  99.8 21.6 %collective-permute-done.1.rest_2_ = bf16[8,2,32,1024]{3,2,1,0:T(8,128)(2,1)} collective-permute-done((bf16[8,2,32,1024]{3,2,1,0:T(8,128)(2,1)}, bf16[8,2,32,1024]{3,2,1,0:T(8,128)(2,1)}, u32[]{:S(2)}, u32[]{:S(2)}) %collective-permute-start.1) | collective-permute-done | bytes 1048608 | tf_op jit(solution)/shard_map/ppermute | solution.py:287
  121.7 32.2 %form_beams.8 = (bf16[8,2,8,64,128]{4,3,2,1,0:T(8,128)(2,1)}, f32[8,32,1024]{2,1,0:T(8,128)S(1)}) custom-call(f32[8]{0:T(128)S(1)} %get-tuple-element.213.freq_ref, s32[4]{0:T(128)S(1)} %iota_xor_fusion.source_ref, bf16[8,2,32,1024]{3,2,1,0:T(8,128)(2,1)S(1)} %get-tuple-element.84.rest_0_, bf16[8,2,32,1024]{3,2,1,0:T(8,128)(2,1)} %collective-permute-done.rest_1_, ...), custom_call_target="tpu_custom_call" | custom-call | flops 11811160064 | bytes 8388608 | tf_op jit(solution)/shard_map/form_beams/pallas_call | solution.py:206
  154.9 4.9 all-to-all-start
  167.4 18.6 %collective-permute-done.3.rest_1_ = bf16[8,2,32,1024]{3,2,1,0:T(8,128)(2,1)S(1)} collective-permute-done((bf16[8,2,32,1024]{3,2,1,0:T(8,128)(2,1)}, bf16[8,2,32,1024]{3,2,1,0:T(8,128)(2,1)S(1)}, u32[]{:S(2)}, u32[]{:S(2)}) %collective-permute-start.3) | collective-permute-done | bytes 1048608 | tf_op jit(solution)/shard_map/ppermute | solution.py:287
  186.0 23.3 %collective-permute-done.4.rest_2_ = bf16[8,2,32,1024]{3,2,1,0:T(8,128)(2,1)S(1)} collective-permute-done((bf16[8,2,32,1024]{3,2,1,0:T(8,128)(2,1)}, bf16[8,2,32,1024]{3,2,1,0:T(8,128)(2,1)S(1)}, u32[]{:S(2)}, u32[]{:S(2)}) %collective-permute-start.4) | collective-permute-done | bytes 1048608 | tf_op jit(solution)/shard_map/ppermute | solution.py:287
  209.3 31.5 %form_beams.9 = (bf16[8,2,8,64,128]{4,3,2,1,0:T(8,128)(2,1)}, f32[8,32,1024]{2,1,0:T(8,128)S(1)}) custom-call(f32[8]{0:T(128)S(1)} %get-tuple-element.212.freq_ref, s32[4]{0:T(128)S(1)} %iota_xor_fusion.source_ref, bf16[8,2,32,1024]{3,2,1,0:T(8,128)(2,1)S(1)} %get-tuple-element.94.rest_0_, bf16[8,2,32,1024]{3,2,1,0:T(8,128)(2,1)S(1)} %collective-permute-done.3.rest_1_, ...), custom_call_target="tpu_custom_call" | custom-call | flops 11811160064 | bytes 8388608 | tf_op jit(solution)/shard_map/form_beams/pallas_call | solution.py:206
  254.1 18.5 %collective-permute-done.6.rest_1_ = bf16[8,2,32,1024]{3,2,1,0:T(8,128)(2,1)S(1)} collective-permute-done((bf16[8,2,32,1024]{3,2,1,0:T(8,128)(2,1)}, bf16[8,2,32,1024]{3,2,1,0:T(8,128)(2,1)S(1)}, u32[]{:S(2)}, u32[]{:S(2)}) %collective-permute-start.6) | collective-permute-done | bytes 1048608 | tf_op jit(solution)/shard_map/ppermute | solution.py:287
  272.9 22.1 %collective-permute-done.8.rest_3_ = bf16[8,2,32,1024]{3,2,1,0:T(8,128)(2,1)S(1)} collective-permute-done((bf16[8,2,32,1024]{3,2,1,0:T(8,128)(2,1)}, bf16[8,2,32,1024]{3,2,1,0:T(8,128)(2,1)S(1)}, u32[]{:S(2)}, u32[]{:S(2)}) %collective-permute-start.8) | collective-permute-done | bytes 1048608 | tf_op jit(solution)/shard_map/ppermute | solution.py:287
  295.0 31.3 %form_beams.10 = (bf16[8,2,8,64,128]{4,3,2,1,0:T(8,128)(2,1)}, f32[8,32,1024]{2,1,0:T(8,128)S(1)}) custom-call(f32[8]{0:T(128)S(1)} %get-tuple-element.211.freq_ref, s32[4]{0:T(128)S(1)} %iota_xor_fusion.source_ref, bf16[8,2,32,1024]{3,2,1,0:T(8,128)(2,1)S(1)} %get-tuple-element.104.rest_0_, bf16[8,2,32,1024]{3,2,1,0:T(8,128)(2,1)S(1)} %collective-permute-done.6.rest_1_, ...), custom_call_target="tpu_custom_call" | custom-call | flops 11811160064 | bytes 8388608 | tf_op jit(solution)/shard_map/form_beams/pallas_call | solution.py:206
  339.5 18.6 %collective-permute-done.9.rest_1_ = bf16[8,2,32,1024]{3,2,1,0:T(8,128)(2,1)S(1)} collective-permute-done((bf16[8,2,32,1024]{3,2,1,0:T(8,128)(2,1)}, bf16[8,2,32,1024]{3,2,1,0:T(8,128)(2,1)S(1)}, u32[]{:S(2)}, u32[]{:S(2)}) %collective-permute-start.9) | collective-permute-done | bytes 1048608 | tf_op jit(solution)/shard_map/ppermute | solution.py:287
  358.1 23.3 %collective-permute-done.10.rest_2_ = bf16[8,2,32,1024]{3,2,1,0:T(8,128)(2,1)S(1)} collective-permute-done((bf16[8,2,32,1024]{3,2,1,0:T(8,128)(2,1)}, bf16[8,2,32,1024]{3,2,1,0:T(8,128)(2,1)S(1)}, u32[]{:S(2)}, u32[]{:S(2)}) %collective-permute-start.10) | collective-permute-done | bytes 1048608 | tf_op jit(solution)/shard_map/ppermute | solution.py:287
  381.4 31.5 %form_beams.11 = (bf16[8,2,8,64,128]{4,3,2,1,0:T(8,128)(2,1)}, f32[8,32,1024]{2,1,0:T(8,128)S(1)}) custom-call(f32[8]{0:T(128)S(1)} %get-tuple-element.210.freq_ref, s32[4]{0:T(128)S(1)} %iota_xor_fusion.source_ref, bf16[8,2,32,1024]{3,2,1,0:T(8,128)(2,1)S(1)} %get-tuple-element.114.rest_0_, bf16[8,2,32,1024]{3,2,1,0:T(8,128)(2,1)S(1)} %collective-permute-done.9.rest_1_, ...), custom_call_target="tpu_custom_call" | custom-call | flops 11811160064 | bytes 8388608 | tf_op jit(solution)/shard_map/form_beams/pallas_call | solution.py:206
  413.9 4.9 all-to-all-start.3
  426.4 18.5 %collective-permute-done.12.rest_1_ = bf16[8,2,32,1024]{3,2,1,0:T(8,128)(2,1)S(1)} collective-permute-done((bf16[8,2,32,1024]{3,2,1,0:T(8,128)(2,1)}, bf16[8,2,32,1024]{3,2,1,0:T(8,128)(2,1)S(1)}, u32[]{:S(2)}, u32[]{:S(2)}) %collective-permute-start.12) | collective-permute-done | bytes 1048608 | tf_op jit(solution)/shard_map/ppermute | solution.py:287
  445.2 22.1 %collective-permute-done.14.rest_3_ = bf16[8,2,32,1024]{3,2,1,0:T(8,128)(2,1)S(1)} collective-permute-done((bf16[8,2,32,1024]{3,2,1,0:T(8,128)(2,1)}, bf16[8,2,32,1024]{3,2,1,0:T(8,128)(2,1)S(1)}, u32[]{:S(2)}, u32[]{:S(2)}) %collective-permute-start.14) | collective-permute-done | bytes 1048608 | tf_op jit(solution)/shard_map/ppermute | solution.py:287
  467.2 31.3 %form_beams.12 = (bf16[8,2,8,64,128]{4,3,2,1,0:T(8,128)(2,1)}, f32[8,32,1024]{2,1,0:T(8,128)S(1)}) custom-call(f32[8]{0:T(128)S(1)} %get-tuple-element.209.freq_ref, s32[4]{0:T(128)S(1)} %iota_xor_fusion.source_ref, bf16[8,2,32,1024]{3,2,1,0:T(8,128)(2,1)S(1)} %get-tuple-element.124.rest_0_, bf16[8,2,32,1024]{3,2,1,0:T(8,128)(2,1)S(1)} %collective-permute-done.12.rest_1_, ...), custom_call_target="tpu_custom_call" | custom-call | flops 11811160064 | bytes 8388608 | tf_op jit(solution)/shard_map/form_beams/pallas_call | solution.py:206
  499.5 4.9 all-to-all-start.4
  511.9 18.6 %collective-permute-done.15.rest_1_ = bf16[8,2,32,1024]{3,2,1,0:T(8,128)(2,1)S(1)} collective-permute-done((bf16[8,2,32,1024]{3,2,1,0:T(8,128)(2,1)}, bf16[8,2,32,1024]{3,2,1,0:T(8,128)(2,1)S(1)}, u32[]{:S(2)}, u32[]{:S(2)}) %collective-permute-start.15) | collective-permute-done | bytes 1048608 | tf_op jit(solution)/shard_map/ppermute | solution.py:287
  530.5 23.3 %collective-permute-done.16.rest_2_ = bf16[8,2,32,1024]{3,2,1,0:T(8,128)(2,1)S(1)} collective-permute-done((bf16[8,2,32,1024]{3,2,1,0:T(8,128)(2,1)}, bf16[8,2,32,1024]{3,2,1,0:T(8,128)(2,1)S(1)}, u32[]{:S(2)}, u32[]{:S(2)}) %collective-permute-start.16) | collective-permute-done | bytes 1048608 | tf_op jit(solution)/shard_map/ppermute | solution.py:287
  553.8 31.5 %form_beams.13 = (bf16[8,2,8,64,128]{4,3,2,1,0:T(8,128)(2,1)}, f32[8,32,1024]{2,1,0:T(8,128)S(1)}) custom-call(f32[8]{0:T(128)S(1)} %get-tuple-element.208.freq_ref, s32[4]{0:T(128)S(1)} %iota_xor_fusion.source_ref, bf16[8,2,32,1024]{3,2,1,0:T(8,128)(2,1)S(1)} %get-tuple-element.134.rest_0_, bf16[8,2,32,1024]{3,2,1,0:T(8,128)(2,1)S(1)} %collective-permute-done.15.rest_1_, ...), custom_call_target="tpu_custom_call" | custom-call | flops 11811160064 | bytes 8388608 | tf_op jit(solution)/shard_map/form_beams/pallas_call | solution.py:206
  598.9 18.5 %collective-permute-done.18.rest_1_ = bf16[8,2,32,1024]{3,2,1,0:T(8,128)(2,1)S(1)} collective-permute-done((bf16[8,2,32,1024]{3,2,1,0:T(8,128)(2,1)}, bf16[8,2,32,1024]{3,2,1,0:T(8,128)(2,1)S(1)}, u32[]{:S(2)}, u32[]{:S(2)}) %collective-permute-start.18) | collective-permute-done | bytes 1048608 | tf_op jit(solution)/shard_map/ppermute | solution.py:287
  617.6 22.1 %collective-permute-done.20.rest_3_ = bf16[8,2,32,1024]{3,2,1,0:T(8,128)(2,1)S(1)} collective-permute-done((bf16[8,2,32,1024]{3,2,1,0:T(8,128)(2,1)}, bf16[8,2,32,1024]{3,2,1,0:T(8,128)(2,1)S(1)}, u32[]{:S(2)}, u32[]{:S(2)}) %collective-permute-start.20) | collective-permute-done | bytes 1048608 | tf_op jit(solution)/shard_map/ppermute | solution.py:287
  639.7 31.3 %form_beams.14 = (bf16[8,2,8,64,128]{4,3,2,1,0:T(8,128)(2,1)}, f32[8,32,1024]{2,1,0:T(8,128)S(1)}) custom-call(f32[8]{0:T(128)S(1)} %get-tuple-element.207.freq_ref, s32[4]{0:T(128)S(1)} %iota_xor_fusion.source_ref, bf16[8,2,32,1024]{3,2,1,0:T(8,128)(2,1)S(1)} %get-tuple-element.144.rest_0_, bf16[8,2,32,1024]{3,2,1,0:T(8,128)(2,1)S(1)} %collective-permute-done.18.rest_1_, ...), custom_call_target="tpu_custom_call" | custom-call | flops 11811160064 | bytes 8388608 | tf_op jit(solution)/shard_map/form_beams/pallas_call | solution.py:206
  680.2 22.7 %collective-permute-done.21.rest_1_ = bf16[8,2,32,1024]{3,2,1,0:T(8,128)(2,1)S(1)} collective-permute-done((bf16[8,2,32,1024]{3,2,1,0:T(8,128)(2,1)}, bf16[8,2,32,1024]{3,2,1,0:T(8,128)(2,1)S(1)}, u32[]{:S(2)}, u32[]{:S(2)}) %collective-permute-start.21) | collective-permute-done | bytes 1048608 | tf_op jit(solution)/shard_map/ppermute | solution.py:287
  702.9 23.3 %collective-permute-done.22.rest_2_ = bf16[8,2,32,1024]{3,2,1,0:T(8,128)(2,1)S(1)} collective-permute-done((bf16[8,2,32,1024]{3,2,1,0:T(8,128)(2,1)}, bf16[8,2,32,1024]{3,2,1,0:T(8,128)(2,1)S(1)}, u32[]{:S(2)}, u32[]{:S(2)}) %collective-permute-start.22) | collective-permute-done | bytes 1048608 | tf_op jit(solution)/shard_map/ppermute | solution.py:287
  727.3 31.4 %form_beams.15 = (bf16[8,2,8,64,128]{4,3,2,1,0:T(8,128)(2,1)}, f32[8,32,1024]{2,1,0:T(8,128)S(1)}) custom-call(f32[8]{0:T(128)S(1)} %get-tuple-element.206.freq_ref, s32[4]{0:T(128)S(1)} %iota_xor_fusion.source_ref, bf16[8,2,32,1024]{3,2,1,0:T(8,128)(2,1)S(1)} %get-tuple-element.149.rest_0_, bf16[8,2,32,1024]{3,2,1,0:T(8,128)(2,1)S(1)} %collective-permute-done.21.rest_1_, ...), custom_call_target="tpu_custom_call" | custom-call | flops 11811160064 | bytes 8388608 | tf_op jit(solution)/shard_map/form_beams/pallas_call | solution.py:206
  759.7 4.9 all-to-all-start.7
  794.6 19.1 %all-to-all-done.7 = bf16[8,2,8,64,128]{4,3,2,1,0:T(8,128)(2,1)} async-done(((bf16[8,2,8,64,128]{4,3,2,1,0:T(8,128)(2,1)}), bf16[8,2,8,64,128]{4,3,2,1,0:T(8,128)(2,1)}, u32[]{:S(2)}, u32[]{:S(2)}) %all-to-all-start.7) | async-done | bytes 2097184 | tf_op jit(solution)/shard_map/all_to_all | solution.py:276
  817.2 13.9 %copy.8 = bf16[2,8,64,64,128]{4,3,2,1,0:T(8,128)(2,1)} copy(bf16[2,8,64,64,128]{4,3,2,0,1:T(8,128)(2,1)} %bitcast.45) | data formatting | bytes 33554432
  (129 shorter events, 128.6 us)
Async XLA Ops:
  71.6 28.2 %collective-permute-start.2 = (bf16[8,2,32,1024]{3,2,1,0:T(8,128)(2,1)}, bf16[8,2,32,1024]{3,2,1,0:T(8,128)(2,1)}, u32[]{:S(2)}, u32[]{:S(2)}) collective-permute-start(bf16[8,2,32,1024]{3,2,1,0:T(8,128)(2,1)} %get-tuple-element.198), channel_id=1, source_target_pairs={{0,24},{8,16},{16,8},{24,0},{1,25},{9,17},{17,9},{25,1},{2,26},{10... | collective-permute-start | bytes 3145736 | tf_op jit(solution)/shard_map/ppermute | solution.py:287
  75.5 45.9 %collective-permute-start.1 = (bf16[8,2,32,1024]{3,2,1,0:T(8,128)(2,1)}, bf16[8,2,32,1024]{3,2,1,0:T(8,128)(2,1)}, u32[]{:S(2)}, u32[]{:S(2)}) collective-permute-start(bf16[8,2,32,1024]{3,2,1,0:T(8,128)(2,1)} %get-tuple-element.199), channel_id=1, source_target_pairs={{0,16},{8,24},{16,0},{24,8},{1,17},{9,25},{17,1},{25,9},{2,18},{10... | collective-permute-start | bytes 3145736 | tf_op jit(solution)/shard_map/ppermute | solution.py:287
  76.0 45.7 %collective-permute-start = (bf16[8,2,32,1024]{3,2,1,0:T(8,128)(2,1)}, bf16[8,2,32,1024]{3,2,1,0:T(8,128)(2,1)}, u32[]{:S(2)}, u32[]{:S(2)}) collective-permute-start(bf16[8,2,32,1024]{3,2,1,0:T(8,128)(2,1)} %get-tuple-element.200), channel_id=1, source_target_pairs={{0,8},{8,0},{16,24},{24,16},{1,9},{9,1},{17,25},{25,17},{2,10},{10... | collective-permute-start | bytes 3145736 | tf_op jit(solution)/shard_map/ppermute | solution.py:287
  154.9 86.8 %all-to-all-start = ((bf16[8,2,8,64,128]{4,3,2,1,0:T(8,128)(2,1)}), bf16[8,2,8,64,128]{4,3,2,1,0:T(8,128)(2,1)}, u32[]{:S(2)}, u32[]{:S(2)}) async-start(bf16[8,2,8,64,128]{4,3,2,1,0:T(8,128)(2,1)} %get-tuple-element.88), calls=%async_computation | async-start | bytes 4194304 | tf_op jit(solution)/shard_map/all_to_all | solution.py:276
  159.8 26.2 %collective-permute-start.3 = (bf16[8,2,32,1024]{3,2,1,0:T(8,128)(2,1)}, bf16[8,2,32,1024]{3,2,1,0:T(8,128)(2,1)S(1)}, u32[]{:S(2)}, u32[]{:S(2)}) collective-permute-start(bf16[8,2,32,1024]{3,2,1,0:T(8,128)(2,1)} %get-tuple-element.91), channel_id=1, source_target_pairs={{0,8},{8,0},{16,24},{24,16},{1,9},{9,1},{17,25},{25,17},{2,10},{10... | collective-permute-start | bytes 3145736 | tf_op jit(solution)/shard_map/ppermute | solution.py:287
  161.3 48.0 %collective-permute-start.4 = (bf16[8,2,32,1024]{3,2,1,0:T(8,128)(2,1)}, bf16[8,2,32,1024]{3,2,1,0:T(8,128)(2,1)S(1)}, u32[]{:S(2)}, u32[]{:S(2)}) collective-permute-start(bf16[8,2,32,1024]{3,2,1,0:T(8,128)(2,1)} %get-tuple-element.92), channel_id=1, source_target_pairs={{0,16},{8,24},{16,0},{24,8},{1,17},{9,25},{17,1},{25,9},{2,18},{10... | collective-permute-start | bytes 3145736 | tf_op jit(solution)/shard_map/ppermute | solution.py:287
  162.0 47.3 %collective-permute-start.5 = (bf16[8,2,32,1024]{3,2,1,0:T(8,128)(2,1)}, bf16[8,2,32,1024]{3,2,1,0:T(8,128)(2,1)S(1)}, u32[]{:S(2)}, u32[]{:S(2)}) collective-permute-start(bf16[8,2,32,1024]{3,2,1,0:T(8,128)(2,1)} %get-tuple-element.93), channel_id=1, source_target_pairs={{0,24},{8,16},{16,8},{24,0},{1,25},{9,17},{17,9},{25,1},{2,26},{10... | collective-permute-start | bytes 3145736 | tf_op jit(solution)/shard_map/ppermute | solution.py:287
  241.7 85.5 %all-to-all-start.1 = ((bf16[8,2,8,64,128]{4,3,2,1,0:T(8,128)(2,1)}), bf16[8,2,8,64,128]{4,3,2,1,0:T(8,128)(2,1)}, u32[]{:S(2)}, u32[]{:S(2)}) async-start(bf16[8,2,8,64,128]{4,3,2,1,0:T(8,128)(2,1)} %get-tuple-element.98), calls=%async_computation.1 | async-start | bytes 4194304 | tf_op jit(solution)/shard_map/all_to_all | solution.py:276
  246.5 26.2 %collective-permute-start.6 = (bf16[8,2,32,1024]{3,2,1,0:T(8,128)(2,1)}, bf16[8,2,32,1024]{3,2,1,0:T(8,128)(2,1)S(1)}, u32[]{:S(2)}, u32[]{:S(2)}) collective-permute-start(bf16[8,2,32,1024]{3,2,1,0:T(8,128)(2,1)} %get-tuple-element.101), channel_id=1, source_target_pairs={{0,8},{8,0},{16,24},{24,16},{1,9},{9,1},{17,25},{25,17},{2,10},{10... | collective-permute-start | bytes 3145736 | tf_op jit(solution)/shard_map/ppermute | solution.py:287
  247.0 25.9 %collective-permute-start.7 = (bf16[8,2,32,1024]{3,2,1,0:T(8,128)(2,1)}, bf16[8,2,32,1024]{3,2,1,0:T(8,128)(2,1)S(1)}, u32[]{:S(2)}, u32[]{:S(2)}) collective-permute-start(bf16[8,2,32,1024]{3,2,1,0:T(8,128)(2,1)} %get-tuple-element.102), channel_id=1, source_target_pairs={{0,16},{8,24},{16,0},{24,8},{1,17},{9,25},{17,1},{25,9},{2,18},{10... | collective-permute-start | bytes 3145736 | tf_op jit(solution)/shard_map/ppermute | solution.py:287
  248.4 46.5 %collective-permute-start.8 = (bf16[8,2,32,1024]{3,2,1,0:T(8,128)(2,1)}, bf16[8,2,32,1024]{3,2,1,0:T(8,128)(2,1)S(1)}, u32[]{:S(2)}, u32[]{:S(2)}) collective-permute-start(bf16[8,2,32,1024]{3,2,1,0:T(8,128)(2,1)} %get-tuple-element.103), channel_id=1, source_target_pairs={{0,24},{8,16},{16,8},{24,0},{1,25},{9,17},{17,9},{25,1},{2,26},{10... | collective-permute-start | bytes 3145736 | tf_op jit(solution)/shard_map/ppermute | solution.py:287
  327.2 86.7 %all-to-all-start.2 = ((bf16[8,2,8,64,128]{4,3,2,1,0:T(8,128)(2,1)}), bf16[8,2,8,64,128]{4,3,2,1,0:T(8,128)(2,1)}, u32[]{:S(2)}, u32[]{:S(2)}) async-start(bf16[8,2,8,64,128]{4,3,2,1,0:T(8,128)(2,1)} %get-tuple-element.108), calls=%async_computation.2 | async-start | bytes 4194304 | tf_op jit(solution)/shard_map/all_to_all | solution.py:276
  331.9 26.2 %collective-permute-start.9 = (bf16[8,2,32,1024]{3,2,1,0:T(8,128)(2,1)}, bf16[8,2,32,1024]{3,2,1,0:T(8,128)(2,1)S(1)}, u32[]{:S(2)}, u32[]{:S(2)}) collective-permute-start(bf16[8,2,32,1024]{3,2,1,0:T(8,128)(2,1)} %get-tuple-element.111), channel_id=1, source_target_pairs={{0,8},{8,0},{16,24},{24,16},{1,9},{9,1},{17,25},{25,17},{2,10},{10... | collective-permute-start | bytes 3145736 | tf_op jit(solution)/shard_map/ppermute | solution.py:287
  333.4 48.0 %collective-permute-start.10 = (bf16[8,2,32,1024]{3,2,1,0:T(8,128)(2,1)}, bf16[8,2,32,1024]{3,2,1,0:T(8,128)(2,1)S(1)}, u32[]{:S(2)}, u32[]{:S(2)}) collective-permute-start(bf16[8,2,32,1024]{3,2,1,0:T(8,128)(2,1)} %get-tuple-element.112), channel_id=1, source_target_pairs={{0,16},{8,24},{16,0},{24,8},{1,17},{9,25},{17,1},{25,9},{2,18},{10... | collective-permute-start | bytes 3145736 | tf_op jit(solution)/shard_map/ppermute | solution.py:287
  334.2 47.3 %collective-permute-start.11 = (bf16[8,2,32,1024]{3,2,1,0:T(8,128)(2,1)}, bf16[8,2,32,1024]{3,2,1,0:T(8,128)(2,1)S(1)}, u32[]{:S(2)}, u32[]{:S(2)}) collective-permute-start(bf16[8,2,32,1024]{3,2,1,0:T(8,128)(2,1)} %get-tuple-element.113), channel_id=1, source_target_pairs={{0,24},{8,16},{16,8},{24,0},{1,25},{9,17},{17,9},{25,1},{2,26},{10... | collective-permute-start | bytes 3145736 | tf_op jit(solution)/shard_map/ppermute | solution.py:287
  413.9 85.6 %all-to-all-start.3 = ((bf16[8,2,8,64,128]{4,3,2,1,0:T(8,128)(2,1)}), bf16[8,2,8,64,128]{4,3,2,1,0:T(8,128)(2,1)}, u32[]{:S(2)}, u32[]{:S(2)}) async-start(bf16[8,2,8,64,128]{4,3,2,1,0:T(8,128)(2,1)} %get-tuple-element.118), calls=%async_computation.3 | async-start | bytes 4194304 | tf_op jit(solution)/shard_map/all_to_all | solution.py:276
  418.8 26.2 %collective-permute-start.12 = (bf16[8,2,32,1024]{3,2,1,0:T(8,128)(2,1)}, bf16[8,2,32,1024]{3,2,1,0:T(8,128)(2,1)S(1)}, u32[]{:S(2)}, u32[]{:S(2)}) collective-permute-start(bf16[8,2,32,1024]{3,2,1,0:T(8,128)(2,1)} %get-tuple-element.121), channel_id=1, source_target_pairs={{0,8},{8,0},{16,24},{24,16},{1,9},{9,1},{17,25},{25,17},{2,10},{10... | collective-permute-start | bytes 3145736 | tf_op jit(solution)/shard_map/ppermute | solution.py:287
  419.3 25.9 %collective-permute-start.13 = (bf16[8,2,32,1024]{3,2,1,0:T(8,128)(2,1)}, bf16[8,2,32,1024]{3,2,1,0:T(8,128)(2,1)S(1)}, u32[]{:S(2)}, u32[]{:S(2)}) collective-permute-start(bf16[8,2,32,1024]{3,2,1,0:T(8,128)(2,1)} %get-tuple-element.122), channel_id=1, source_target_pairs={{0,16},{8,24},{16,0},{24,8},{1,17},{9,25},{17,1},{25,9},{2,18},{10... | collective-permute-start | bytes 3145736 | tf_op jit(solution)/shard_map/ppermute | solution.py:287
  420.7 46.5 %collective-permute-start.14 = (bf16[8,2,32,1024]{3,2,1,0:T(8,128)(2,1)}, bf16[8,2,32,1024]{3,2,1,0:T(8,128)(2,1)S(1)}, u32[]{:S(2)}, u32[]{:S(2)}) collective-permute-start(bf16[8,2,32,1024]{3,2,1,0:T(8,128)(2,1)} %get-tuple-element.123), channel_id=1, source_target_pairs={{0,24},{8,16},{16,8},{24,0},{1,25},{9,17},{17,9},{25,1},{2,26},{10... | collective-permute-start | bytes 3145736 | tf_op jit(solution)/shard_map/ppermute | solution.py:287
  499.5 86.9 %all-to-all-start.4 = ((bf16[8,2,8,64,128]{4,3,2,1,0:T(8,128)(2,1)}), bf16[8,2,8,64,128]{4,3,2,1,0:T(8,128)(2,1)}, u32[]{:S(2)}, u32[]{:S(2)}) async-start(bf16[8,2,8,64,128]{4,3,2,1,0:T(8,128)(2,1)} %get-tuple-element.128), calls=%async_computation.4 | async-start | bytes 4194304 | tf_op jit(solution)/shard_map/all_to_all | solution.py:276
  504.3 26.2 %collective-permute-start.15 = (bf16[8,2,32,1024]{3,2,1,0:T(8,128)(2,1)}, bf16[8,2,32,1024]{3,2,1,0:T(8,128)(2,1)S(1)}, u32[]{:S(2)}, u32[]{:S(2)}) collective-permute-start(bf16[8,2,32,1024]{3,2,1,0:T(8,128)(2,1)} %get-tuple-element.131), channel_id=1, source_target_pairs={{0,8},{8,0},{16,24},{24,16},{1,9},{9,1},{17,25},{25,17},{2,10},{10... | collective-permute-start | bytes 3145736 | tf_op jit(solution)/shard_map/ppermute | solution.py:287
  505.9 48.0 %collective-permute-start.16 = (bf16[8,2,32,1024]{3,2,1,0:T(8,128)(2,1)}, bf16[8,2,32,1024]{3,2,1,0:T(8,128)(2,1)S(1)}, u32[]{:S(2)}, u32[]{:S(2)}) collective-permute-start(bf16[8,2,32,1024]{3,2,1,0:T(8,128)(2,1)} %get-tuple-element.132), channel_id=1, source_target_pairs={{0,16},{8,24},{16,0},{24,8},{1,17},{9,25},{17,1},{25,9},{2,18},{10... | collective-permute-start | bytes 3145736 | tf_op jit(solution)/shard_map/ppermute | solution.py:287
  506.6 47.3 %collective-permute-start.17 = (bf16[8,2,32,1024]{3,2,1,0:T(8,128)(2,1)}, bf16[8,2,32,1024]{3,2,1,0:T(8,128)(2,1)S(1)}, u32[]{:S(2)}, u32[]{:S(2)}) collective-permute-start(bf16[8,2,32,1024]{3,2,1,0:T(8,128)(2,1)} %get-tuple-element.133), channel_id=1, source_target_pairs={{0,24},{8,16},{16,8},{24,0},{1,25},{9,17},{17,9},{25,1},{2,26},{10... | collective-permute-start | bytes 3145736 | tf_op jit(solution)/shard_map/ppermute | solution.py:287
  586.4 85.6 %all-to-all-start.5 = ((bf16[8,2,8,64,128]{4,3,2,1,0:T(8,128)(2,1)}), bf16[8,2,8,64,128]{4,3,2,1,0:T(8,128)(2,1)}, u32[]{:S(2)}, u32[]{:S(2)}) async-start(bf16[8,2,8,64,128]{4,3,2,1,0:T(8,128)(2,1)} %get-tuple-element.138), calls=%async_computation.5 | async-start | bytes 4194304 | tf_op jit(solution)/shard_map/all_to_all | solution.py:276
  591.2 26.2 %collective-permute-start.18 = (bf16[8,2,32,1024]{3,2,1,0:T(8,128)(2,1)}, bf16[8,2,32,1024]{3,2,1,0:T(8,128)(2,1)S(1)}, u32[]{:S(2)}, u32[]{:S(2)}) collective-permute-start(bf16[8,2,32,1024]{3,2,1,0:T(8,128)(2,1)} %get-tuple-element.141), channel_id=1, source_target_pairs={{0,8},{8,0},{16,24},{24,16},{1,9},{9,1},{17,25},{25,17},{2,10},{10... | collective-permute-start | bytes 3145736 | tf_op jit(solution)/shard_map/ppermute | solution.py:287
  591.7 25.9 %collective-permute-start.19 = (bf16[8,2,32,1024]{3,2,1,0:T(8,128)(2,1)}, bf16[8,2,32,1024]{3,2,1,0:T(8,128)(2,1)S(1)}, u32[]{:S(2)}, u32[]{:S(2)}) collective-permute-start(bf16[8,2,32,1024]{3,2,1,0:T(8,128)(2,1)} %get-tuple-element.142), channel_id=1, source_target_pairs={{0,16},{8,24},{16,0},{24,8},{1,17},{9,25},{17,1},{25,9},{2,18},{10... | collective-permute-start | bytes 3145736 | tf_op jit(solution)/shard_map/ppermute | solution.py:287
  593.2 46.5 %collective-permute-start.20 = (bf16[8,2,32,1024]{3,2,1,0:T(8,128)(2,1)}, bf16[8,2,32,1024]{3,2,1,0:T(8,128)(2,1)S(1)}, u32[]{:S(2)}, u32[]{:S(2)}) collective-permute-start(bf16[8,2,32,1024]{3,2,1,0:T(8,128)(2,1)} %get-tuple-element.143), channel_id=1, source_target_pairs={{0,24},{8,16},{16,8},{24,0},{1,25},{9,17},{17,9},{25,1},{2,26},{10... | collective-permute-start | bytes 3145736 | tf_op jit(solution)/shard_map/ppermute | solution.py:287
  672.0 87.7 %all-to-all-start.6 = ((bf16[8,2,8,64,128]{4,3,2,1,0:T(8,128)(2,1)}), bf16[8,2,8,64,128]{4,3,2,1,0:T(8,128)(2,1)}, u32[]{:S(2)}, u32[]{:S(2)}) async-start(bf16[8,2,8,64,128]{4,3,2,1,0:T(8,128)(2,1)} %get-tuple-element.148), calls=%async_computation.6 | async-start | bytes 4194304 | tf_op jit(solution)/shard_map/all_to_all | solution.py:276
  676.7 26.2 %collective-permute-start.21 = (bf16[8,2,32,1024]{3,2,1,0:T(8,128)(2,1)}, bf16[8,2,32,1024]{3,2,1,0:T(8,128)(2,1)S(1)}, u32[]{:S(2)}, u32[]{:S(2)}) collective-permute-start(bf16[8,2,32,1024]{3,2,1,0:T(8,128)(2,1)} %get-tuple-element.150), channel_id=1, source_target_pairs={{0,8},{8,0},{16,24},{24,16},{1,9},{9,1},{17,25},{25,17},{2,10},{10... | collective-permute-start | bytes 3145736 | tf_op jit(solution)/shard_map/ppermute | solution.py:287
  678.2 48.0 %collective-permute-start.22 = (bf16[8,2,32,1024]{3,2,1,0:T(8,128)(2,1)}, bf16[8,2,32,1024]{3,2,1,0:T(8,128)(2,1)S(1)}, u32[]{:S(2)}, u32[]{:S(2)}) collective-permute-start(bf16[8,2,32,1024]{3,2,1,0:T(8,128)(2,1)} %get-tuple-element.151), channel_id=1, source_target_pairs={{0,16},{8,24},{16,0},{24,8},{1,17},{9,25},{17,1},{25,9},{2,18},{10... | collective-permute-start | bytes 3145736 | tf_op jit(solution)/shard_map/ppermute | solution.py:287
  679.0 47.3 %collective-permute-start.23 = (bf16[8,2,32,1024]{3,2,1,0:T(8,128)(2,1)}, bf16[8,2,32,1024]{3,2,1,0:T(8,128)(2,1)S(1)}, u32[]{:S(2)}, u32[]{:S(2)}) collective-permute-start(bf16[8,2,32,1024]{3,2,1,0:T(8,128)(2,1)} %get-tuple-element.152), channel_id=1, source_target_pairs={{0,24},{8,16},{16,8},{24,0},{1,25},{9,17},{17,9},{25,1},{2,26},{10... | collective-permute-start | bytes 3145736 | tf_op jit(solution)/shard_map/ppermute | solution.py:287
  759.7 54.1 %all-to-all-start.7 = ((bf16[8,2,8,64,128]{4,3,2,1,0:T(8,128)(2,1)}), bf16[8,2,8,64,128]{4,3,2,1,0:T(8,128)(2,1)}, u32[]{:S(2)}, u32[]{:S(2)}) async-start(bf16[8,2,8,64,128]{4,3,2,1,0:T(8,128)(2,1)} %get-tuple-element.153), calls=%async_computation.7 | async-start | bytes 4194304 | tf_op jit(solution)/shard_map/all_to_all | solution.py:276
  (25 other events, 614.4 us)
